TPU v7x, 32 devices: a whole 2x2x4 slice. The times are simulated.
32 devices in a mesh: seq: 16 (over z, y, x), dp: 2 (over core).
Axes of the slice: x: 2, y: 2, z: 4, core: 2. Of those that a mesh axis runs over, the one named last changes fastest.
Arguments:
- tokens: bfloat16 [4096, 4096], P(('dp', 'seq')), parts along dimension 0, may hold values from -6 to 6
- sign_in: int32 [4096, 256], P(('dp', 'seq')), parts along dimension 0, may hold values from 0 to 65535
- sign_out: int32 [4096, 32], P(('dp', 'seq')), parts along dimension 0, may hold values from 0 to 65535
- w_value: bfloat16 [4096, 512], P('seq'), may hold values from -0.09375 to 0.09375
- w_noise: bfloat16 [4096, 512], P('seq'), may hold values from -0.046875 to 0.046875
- w_gate: bfloat16 [4096, 512], replicated, may hold values from -0.09375 to 0.09375
- conv_taps: float32 [3, 1024], replicated, may hold values from -3.5 to 3.5
- long_filter: float32 [2048, 512], P('seq'), may hold values from -1.5 to 1.5, as said below
- w_out: bfloat16 [512, 4096], replicated, may hold values from -0.25 to 0.25
Outputs:
- mixed: bfloat16 [4096, 4096], P(('dp', 'seq')), parts along dimension 0
There are 2 independent parts, one for each index of `dp`. A program takes and returns all parts, laid end to end along the dimension named above; an argument that names none is the same for every part. Nothing has to cross between parts.
Inputs may be any that keep to these rules, and one draw needn't show every extreme that they name: `long_filter`: filter taps are real and finite.
All inputs are finite; a program needn't handle non-finite values.
Results may differ from a plain program's by a relative error of at most 0.0064.
Values may be sent and summed in bfloat16 or wider, within the bound.
No kernel may reach another device: no remote copies, remote signals or barrier semaphores. Data moves between devices by JAX's collectives and lax.ppermute only.
A program may use at most 64 MiB of HBM per device.

v0:
```python
import functools

import jax
import jax.numpy as jnp
from jax import lax
from jax.experimental import pallas as pl
from jax.experimental.pallas import tpu as pltpu
from jax.sharding import Mesh, PartitionSpec as P

F32 = jnp.float32
BF16 = jnp.bfloat16
LANES = 128
GROUP = 8
BLOCK = 32
SLOTS = LANES // BLOCK
MIB = 1 << 20
VMEM = pl.BlockSpec(memory_space=pltpu.VMEM)
SMEM = pl.BlockSpec(memory_space=pltpu.SMEM)
HBM = pl.BlockSpec(memory_space=pltpu.HBM)
ANY = pl.BlockSpec(memory_space=pl.ANY)


def params(mib):
    return pltpu.CompilerParams(vmem_limit_bytes=mib * MIB)


def cost(flops, accessed):
    return pl.CostEstimate(flops=flops, bytes_accessed=accessed, transcendentals=0)


def in_hbm(*arrays):
    return [pltpu.with_memory_space_constraint(array, pltpu.HBM) for array in arrays]


def sign_bytes(packed):
    parts = jnp.concatenate([packed & 255, packed >> 8], axis=1)
    return parts.astype(F32).astype(BF16)


def one_hot(rows, columns, source_of):
    at = lax.broadcasted_iota(jnp.int32, (rows, columns), 0)
    column = lax.broadcasted_iota(jnp.int32, (1, columns), 1)
    return (at == source_of(column)).astype(F32).astype(BF16)


def pack_kernel(
    near, far, tokens_ref, in_ref, sent_ref, value_ref, noise_ref, weight_ref, *refs
):
    outs, (in_held, sent_held, read_sems, weight_sems, token_sems) = refs[:near], refs[near:]
    core, far_at, near_at = lax.axis_index("dp"), lax.axis_index("far"), lax.axis_index("near")
    half = weight_ref.shape[1] // 2
    share = weight_ref.shape[0]
    depth = share * far
    words = in_ref.shape[1]
    per_part = words // (near * far)
    own_words = per_part * far

    copies = []
    for at, source in enumerate((value_ref, noise_ref)):
        columns = pl.ds(pl.multiple_of(core * half, half), half)
        target = weight_ref.at[:, at * half : (at + 1) * half]
        copies.append(pltpu.make_async_copy(source.at[:, columns], target, weight_sems.at[at]))
    reads = [
        pltpu.make_async_copy(in_ref, in_held, read_sems.at[0]),
        pltpu.make_async_copy(sent_ref, sent_held, read_sems.at[1]),
    ]
    for step, out in enumerate(outs):
        for turn in range(far):
            start = ((far_at ^ turn) * near + (near_at ^ step)) * share
            columns = pl.ds(pl.multiple_of(start, share), share)
            target = out.at[:, turn * share : (turn + 1) * share]
            copies.append(
                pltpu.make_async_copy(tokens_ref.at[:, columns], target, token_sems.at[step * far + turn])
            )
    for copy in reads + copies:
        copy.start()

    def word_of(column):
        step, rest = column // (2 * own_words), column % (2 * own_words)
        part, word = rest // own_words, rest % own_words
        plane = (word // per_part) ^ far_at
        return part * words + (plane * near + (step ^ near_at)) * per_part + word % per_part

    by_word = one_hot(2 * words, 2 * words, word_of)
    reads[0].wait()
    moved = jnp.dot(sign_bytes(in_held[...]), by_word, preferred_element_type=F32).astype(BF16)
    reads[1].wait()
    sent = sign_bytes(sent_held[...].astype(F32).T.astype(jnp.int32))
    spare = -sent.shape[1] % LANES
    sent = jnp.concatenate([sent, jnp.zeros((sent.shape[0], spare), BF16)], axis=1)
    width = 2 * own_words
    for step, out in enumerate(outs):
        out[:, depth : depth + width] = moved[:, step * width : (step + 1) * width]
        out[:, depth + width :] = sent
    for copy in copies:
        copy.wait()


def spread_signs(pair, byte_of, columns):
    spread = jnp.dot(pair, one_hot(pair.shape[1], columns, byte_of), preferred_element_type=F32)
    mask = 1 << (lax.broadcasted_iota(jnp.int32, (1, columns), 1) & 7)
    return jnp.where((spread.astype(jnp.int32) & mask) != 0, 1.0, -1.0)


def spaced(lines, held):
    if held >= GROUP:
        return lines
    spare = jnp.zeros((GROUP - held, lines.shape[1]), F32)
    split = [lines[at : at + held] for at in range(0, lines.shape[0], held)]
    return jnp.concatenate([part for own in split for part in (own, spare)], axis=0)


def project_kernel(near, far, cores, depth, lags_ref, *refs):
    outs, (whole_ref, lags_held, sem) = refs[-3 - near : -3], refs[-3:]
    chunks, pieces = refs[: near * cores], refs[near * cores : -3 - near]
    core, near_at = lax.axis_index("dp"), lax.axis_index("near")
    rows = chunks[0].shape[0]
    half = pieces[0].shape[1] // 2
    own_lags = lags_ref.at[:, pl.ds(pl.multiple_of(core * half, half), half)]
    read = pltpu.make_async_copy(own_lags, lags_held, sem)
    read.start()
    words = depth // 16
    sent_words = cores * half // 16
    sent_start = depth + 2 * words

    def in_byte(column):
        return (column >> 4) + words * ((column >> 3) & 1)

    def out_byte(column):
        return core * (half // 16) + (column >> 4) + sent_words * ((column >> 3) & 1)

    def joined(start, stop):
        return jnp.concatenate([chunk[:, start:stop] for chunk in chunks], axis=0)

    flip_in = spread_signs(joined(depth, sent_start), in_byte, depth).astype(BF16)
    flip_out = spread_signs(joined(sent_start, sent_start + 2 * sent_words), out_byte, half)
    mean_part, noise_part = 0.0, 0.0
    step = depth // len(pieces)
    for at, piece in enumerate(pieces):
        tokens = joined(at * step, (at + 1) * step)
        flipped = tokens * flip_in[:, at * step : (at + 1) * step]
        mean_part += jnp.dot(tokens, piece[:, :half], preferred_element_type=F32)
        noise_part += jnp.dot(flipped, piece[:, half:], preferred_element_type=F32)
    held = half // (near * far)
    stride = max(held, GROUP)
    value = spaced((mean_part + flip_out * noise_part).T, held)
    for part in range(cores):
        for turn in range(near):
            at = part * near + turn
            target = ((core ^ part) * near + (near_at ^ turn)) * rows
            whole_ref[:, pl.ds(pl.multiple_of(target, rows), rows)] = value[:, at * rows : (at + 1) * rows]
    read.wait()
    whole_ref[:, cores * near * rows :] = spaced(lags_held[...].T, held)
    for turn, out in enumerate(outs):
        for plane in range(far):
            at = pl.multiple_of((plane * near + (near_at ^ turn)) * stride, stride)
            out[plane * held : (plane + 1) * held, :] = whole_ref[pl.ds(at, held), :].astype(BF16)


def sum_kernel(near, far, rows, *refs):
    parts, outs, whole_ref = refs[:near], refs[near : near + far], refs[-1]
    far_at, near_at = lax.axis_index("far"), lax.axis_index("near")
    held = outs[0].shape[0]
    stride = max(held, GROUP)
    span = parts[0].shape[1] - rows
    total = 0.0
    for turn, part in enumerate(parts):
        total += part[:, :span].astype(F32)
        at = pl.multiple_of(span + (near_at ^ turn) * rows, rows)
        whole_ref[:, pl.ds(at, rows)] = spaced(part[:, span:].astype(F32), held)
    whole_ref[:, :span] = spaced(total, held)
    for turn, out in enumerate(outs):
        at = pl.multiple_of((far_at ^ turn) * stride, stride)
        out[...] = whole_ref[pl.ds(at, held), :].astype(BF16)


def shifted(values, steps):
    moved = pltpu.roll(values, steps, 1)
    at = lax.broadcasted_iota(jnp.int32, values.shape, 1)
    return jnp.where(at >= steps, moved, 0.0)


def lane_roll(values, steps):
    return pltpu.roll(values, steps % LANES, values.ndim - 1) if steps % LANES else values


def mix_kernel(near, far, cores, held, taps_ref, *refs):
    parts, (out_ref, left_ref, sums_ref, done_ref, table_ref, lines_ref) = refs[:-6], refs[-6:]
    tiles = out_ref.shape[0] // cores
    block_rows = cores * GROUP
    tile_rows = SLOTS * block_rows
    rows = tiles * tile_rows
    lane = lax.broadcasted_iota(jnp.int32, (1, LANES), 1)
    pair = 2 * LANES
    span = near * LANES

    def padded(lines):
        if held >= GROUP:
            return lines
        return jnp.concatenate([lines, jnp.zeros((GROUP - held, lines.shape[1]), F32)], axis=0)

    for turn, part in enumerate(parts):
        for plane in range(far // len(parts)):
            own = slice(plane * held, (plane + 1) * held)
            target = pl.multiple_of(((lax.axis_index("far") if len(parts) > 1 else plane) ^ turn) * span, span)
            for line in range(cores + 1):
                piece = part[own, line * span : (line + 1) * span]
                lines_ref[line, :, pl.ds(target, span)] = piece.astype(F32)
    half = held * near * far
    position = lax.axis_index("far") * near + lax.axis_index("near")
    first = lax.axis_index("dp") * half + position * held
    channel = lax.broadcasted_iota(jnp.int32, (held, cores * half), 1) - first
    chosen = channel == lax.broadcasted_iota(jnp.int32, (held, cores * half), 0)
    taps = [
        jnp.sum(jnp.where(chosen, taps_ref[lag : lag + 1, : cores * half], 0.0), axis=1, keepdims=True)
        for lag in range(3)
    ]
    signals = []
    for part in range(cores):
        value = lines_ref[part]
        signal = taps[0] * value
        for lag in range(1, 3):
            signal += taps[lag] * shifted(value, lag)
        signals.append(padded(signal))
    lags = padded(lines_ref[cores])

    for group in range(max(held, GROUP) // GROUP):
        own = slice(group * GROUP, (group + 1) * GROUP)
        for at in range(GROUP):
            row = lags[group * GROUP + at : group * GROUP + at + 1, :]
            repeated = jnp.broadcast_to(row, (BLOCK, row.shape[1]))
            turned = pltpu.roll(repeated, 0, 1, stride=1, stride_axis=0)
            column = lax.broadcasted_iota(jnp.int32, repeated.shape, 1)
            lag = lax.broadcasted_iota(jnp.int32, repeated.shape, 0)
            kept = jnp.where(column >= lag, turned, 0.0).astype(BF16)
            table_ref[at * BLOCK : (at + 1) * BLOCK, :] = kept

        stacked = jnp.concatenate(
            [
                signal[own, a * LANES : (a + 1) * LANES]
                for a in range(tiles)
                for signal in signals
            ],
            axis=0,
        )
        slot_of = lax.broadcasted_iota(jnp.int32, stacked.shape, 0) % SLOTS
        turned = stacked
        for slot in range(1, SLOTS):
            turned = jnp.where(slot_of == slot, lane_roll(stacked, BLOCK * slot), turned)
        spread = jnp.stack(
            [
                lane_roll(turned, -BLOCK * slot).reshape(tiles, block_rows, LANES)
                for slot in range(SLOTS)
            ],
            axis=1,
        ).reshape(rows, LANES)
        owner = lax.broadcasted_iota(jnp.int32, (rows, LANES), 0) % GROUP
        for half in range(GROUP // SLOTS):
            kept = jnp.where(owner == lane // BLOCK + half * SLOTS, spread, 0.0)
            left_ref[:, half * LANES : (half + 1) * LANES] = kept.astype(BF16)

        sums_ref[...] = jnp.zeros_like(sums_ref)
        if tiles <= 16:
            for at in range(tiles // 2):
                start = 2 * at * tile_rows
                partial = jnp.dot(
                    left_ref[: rows - start, :],
                    table_ref[:, at * pair : (at + 1) * pair],
                    preferred_element_type=F32,
                )
                sums_ref[start:rows, :] += partial[:, :LANES]
                sums_ref[start + tile_rows : rows, :] += partial[: rows - start - tile_rows, LANES:]
        else:

            def add(at, _):
                partial = jnp.dot(
                    left_ref[...],
                    table_ref[:, pl.ds(pl.multiple_of(at * pair, pair), pair)],
                    preferred_element_type=F32,
                )
                start = pl.multiple_of(2 * at * tile_rows, tile_rows)
                sums_ref[pl.ds(start, rows), :] += partial[:, :LANES]
                sums_ref[pl.ds(start + tile_rows, rows), :] += partial[:, LANES:]
                return 0

            lax.fori_loop(0, tiles // 2, add, 0)

        sums = sums_ref[:rows, :]
        landed = [0.0] * SLOTS
        for part in range(SLOTS):
            late = sums
            if part:
                ahead = jnp.zeros((part * block_rows, LANES), F32)
                late = jnp.concatenate([ahead, sums[: rows - part * block_rows]], axis=0)
            late = late.reshape(tiles, SLOTS, block_rows, LANES)
            for slot in range(SLOTS):
                moved = late[:, slot].reshape(tiles * block_rows, LANES)
                landed[slot] += lane_roll(moved, BLOCK * (slot - part))
        result = 0.0
        for slot in range(SLOTS):
            result += jnp.where(lane // BLOCK == slot, landed[slot], 0.0)
        result = result.reshape(tiles, cores, GROUP, LANES)
        for part in range(cores):
            done_ref[part * tiles : (part + 1) * tiles, own, :] = result[:, part]

    out_ref[...] = done_ref[:, :held, :].astype(BF16)


def out_kernel(
    gate_ref, before_ref, taps_ref, mixed_ref, source_ref, target_ref,
    gate_held, before_held, taps_held, mixed_held, weight_ref, held_ref, small_sems, read_sems, write_sems,
):
    chunks, channels, step = weight_ref.shape
    small = [
        pltpu.make_async_copy(source, target, small_sems.at[at])
        for at, (source, target) in enumerate(
            (
                (gate_ref, gate_held),
                (before_ref, before_held),
                (taps_ref, taps_held),
                (mixed_ref, mixed_held),
            )
        )
    ]
    reads = [
        pltpu.make_async_copy(
            source_ref.at[:, pl.ds(at * step, step)], weight_ref.at[at], read_sems.at[at]
        )
        for at in range(chunks)
    ]
    for copy in small + reads:
        copy.start()
    for copy in small:
        copy.wait()
    gate = gate_held[...].astype(F32)
    extended = jnp.concatenate([before_held[...].astype(F32), gate], axis=0)
    gate_short = taps_held[0:1, channels:] * gate
    for lag in range(1, 3):
        gate_short += taps_held[lag : lag + 1, channels:] * extended[2 - lag : 2 - lag + gate.shape[0]]
    gated = (gate_short * mixed_held[...].astype(F32).T).astype(BF16)
    writes = []
    for at in range(chunks):
        reads[at].wait()
        held_ref[at] = jnp.dot(gated, weight_ref[at], preferred_element_type=F32).astype(BF16)
        columns = target_ref.at[:, pl.ds(at * step, step)]
        writes.append(pltpu.make_async_copy(held_ref.at[at], columns, write_sems.at[at]))
        writes[-1].start()
    for write in writes:
        write.wait()


def exchanged(value, axis, step):
    return lax.ppermute(value, axis, [(i, i ^ step) for i in range(lax.axis_size(axis))])


def on_device(near, far, tokens, sign_in, sign_out, w_value, w_noise, w_gate, conv_taps, long_filter, w_out):
    rows, width = tokens.shape
    channels = w_gate.shape[1]
    cores = lax.axis_size("dp")
    count = near * far
    half = channels // cores
    held = half // count
    share = w_value.shape[0]
    depth = share * far
    length = count * rows
    near_at, core = lax.axis_index("near"), lax.axis_index("dp")

    packed_width = depth + depth // 8 + channels // 8 + -(channels // 8) % LANES
    if share % LANES == 0 and far == 4:
        weights, *chunks = pl.pallas_call(
            functools.partial(pack_kernel, near, far),
            in_specs=[HBM] * 5,
            out_specs=[VMEM] * (1 + near),
            out_shape=[jax.ShapeDtypeStruct((share, 2 * half), BF16)]
            + [jax.ShapeDtypeStruct((rows, packed_width), BF16)] * near,
            scratch_shapes=[
                pltpu.VMEM(sign_in.shape, jnp.int32),
                pltpu.VMEM(sign_out.shape[::-1], jnp.int32),
                pltpu.SemaphoreType.DMA((2,)),
                pltpu.SemaphoreType.DMA((2,)),
                pltpu.SemaphoreType.DMA((near * far,)),
            ],
            compiler_params=params(16),
            cost_estimate=cost(2 * rows * 512 * 512, 3 * MIB),
            name="pack",
        )(*in_hbm(tokens, sign_in, sign_out.T, w_value, w_noise))
        pieces = [weights] * far
        for turn in (2, 1):
            pieces[turn] = exchanged(weights, "far", turn)
    else:
        own = lax.dynamic_slice_in_dim(jnp.stack([w_value, w_noise]), core * half, half, axis=2)
        own = own.transpose(1, 0, 2).reshape(share, 2 * half)
        pieces = [lax.all_gather(own, "far", axis=0, tiled=True)]
        order = jnp.arange(near) ^ near_at

        def by_owner(array):
            parts = array.reshape(rows, far, near, -1).transpose(2, 0, 1, 3).reshape(near, rows, -1)
            return jnp.take(parts, order, axis=0)

        words = by_owner(sign_in)
        sent = jnp.broadcast_to(sign_out[None], (near, *sign_out.shape))
        spare = jnp.zeros((near, rows, -(channels // 8) % LANES), jnp.int32)
        signs = [words & 255, words >> 8, sent & 255, sent >> 8, spare]
        packed = [by_owner(tokens)] + [part.astype(BF16) for part in signs]
        chunks = list(jnp.concatenate(packed, axis=2))
    chunks = [chunks[0]] + [exchanged(chunks[step], "near", step) for step in range(1, near)]

    late_tokens = tokens
    if len(pieces) > 1:
        pieces[1], chunks[0] = lax.optimization_barrier((pieces[1], chunks[0]))
        late_tokens, pieces[2] = lax.optimization_barrier((tokens, pieces[2]))
        pieces[3] = exchanged(pieces[2], "far", 1)
    gate_rows = jnp.dot(late_tokens, w_gate, preferred_element_type=F32).astype(BF16)
    gate_rows, pieces[-1], *chunks[1:] = lax.optimization_barrier((gate_rows, pieces[-1], *chunks[1:]))
    chunks += [exchanged(chunk, "dp", 1) for chunk in chunks]

    near_shape = jax.ShapeDtypeStruct((far * held, (cores * near + 1) * rows), BF16)
    partial = pl.pallas_call(
        functools.partial(project_kernel, near, far, cores, depth),
        in_specs=[HBM] + [VMEM] * (len(chunks) + len(pieces)),
        out_specs=[VMEM] * near,
        out_shape=[near_shape] * near,
        scratch_shapes=[
            pltpu.VMEM((count * max(held, GROUP), near_shape.shape[1]), F32),
            pltpu.VMEM((rows, half), F32),
            pltpu.SemaphoreType.DMA,
        ],
        compiler_params=params(40),
        cost_estimate=cost(4 * cores * near * rows * depth * half, 6 * MIB),
        name="project",
    )(*in_hbm(long_filter), *chunks, *pieces)
    partial = list(partial)
    last_rows, partial[0] = lax.optimization_barrier((gate_rows[rows - 2 :], partial[0]))
    before = lax.ppermute(last_rows, ("far", "near"), [(i, i + 1) for i in range(count - 1)])
    partial = [partial[0]] + [exchanged(partial[step], "near", step) for step in range(1, near)]

    far_shape = (held, (cores + 1) * near * rows)
    parts = pl.pallas_call(
        functools.partial(sum_kernel, near, far, rows),
        in_specs=[VMEM] * near,
        out_specs=[VMEM] * far,
        out_shape=[jax.ShapeDtypeStruct(far_shape, BF16)] * far,
        scratch_shapes=[pltpu.VMEM((far * max(held, GROUP), far_shape[1]), F32)],
        compiler_params=params(16),
        cost_estimate=cost(MIB, MIB),
        name="sum",
    )(*partial)
    if far == 4:
        parts = [parts[0]] + [exchanged(parts[turn], "far", turn) for turn in range(1, far)]
    else:
        order = jnp.arange(far) ^ lax.axis_index("far")
        parts = lax.all_to_all(jnp.take(jnp.stack(parts), order, axis=0), "far", 0, 0, tiled=True)
        parts = [parts.reshape(far * held, far_shape[1])]
    before, parts[0] = lax.optimization_barrier((before, parts[0]))

    tiles = length // LANES
    all_rows = tiles * SLOTS * cores * GROUP
    held_rows = max(held, GROUP)
    mixed = pl.pallas_call(
        functools.partial(mix_kernel, near, far, cores, held),
        in_specs=[VMEM] * (1 + len(parts)),
        out_specs=VMEM,
        out_shape=jax.ShapeDtypeStruct((cores * tiles, held, LANES), BF16),
        scratch_shapes=[
            pltpu.VMEM((all_rows, GROUP * BLOCK), BF16),
            pltpu.VMEM((all_rows * (1 if tiles <= 16 else 2), LANES), F32),
            pltpu.VMEM((cores * tiles, held_rows, LANES), F32),
            pltpu.VMEM((GROUP * BLOCK, length), BF16),
            pltpu.VMEM((cores + 1, held, length), F32),
        ],
        compiler_params=params(48),
        cost_estimate=cost(cores * held_rows * BLOCK * length * 256, 2 * MIB),
        name="mix",
    )(conv_taps, *parts)

    landed = lax.all_to_all(mixed, ("dp", "far", "near"), 0, 0, tiled=True).reshape(channels, rows)
    chunks = 8
    return pl.pallas_call(
        out_kernel,
        in_specs=[ANY] * 4 + [HBM],
        out_specs=HBM,
        out_shape=jax.ShapeDtypeStruct((rows, width), BF16),
        scratch_shapes=[
            pltpu.VMEM(gate_rows.shape, BF16),
            pltpu.VMEM(before.shape, BF16),
            pltpu.VMEM(conv_taps.shape, F32),
            pltpu.VMEM(landed.shape, BF16),
            pltpu.VMEM((chunks, channels, width // chunks), BF16),
            pltpu.VMEM((chunks, rows, width // chunks), BF16),
            pltpu.SemaphoreType.DMA((4,)),
            pltpu.SemaphoreType.DMA((chunks,)),
            pltpu.SemaphoreType.DMA((chunks,)),
        ],
        compiler_params=params(16),
        cost_estimate=cost(2 * rows * width * channels, 5 * MIB),
        name="project_out",
    )(gate_rows, before, conv_taps, landed, *in_hbm(w_out))


def solution(mesh):
    count = mesh.shape["seq"]
    near = 4 if count % 4 == 0 else 1
    far = count // near
    seq_at = mesh.axis_names.index("seq")
    shape = list(mesh.devices.shape)
    shape[seq_at : seq_at + 1] = [far, near]
    names = list(mesh.axis_names)
    names[seq_at : seq_at + 1] = ["far", "near"]
    inner = Mesh(mesh.devices.reshape(shape), tuple(names))
    by_token = P(("dp", "far", "near"), None)
    by_row = P(("far", "near"), None)
    placed = (by_token, by_token, by_token, by_row, by_row, P(), P(), by_row, P())
    return jax.shard_map(
        functools.partial(on_device, near, far),
        mesh=inner,
        in_specs=placed,
        out_specs=by_token,
        check_vma=False,
    )
```

profile of v0, /device:TPU:0, one launch (start us, length us, event | category | flops | bytes accessed | tf_op | source)
XLA Modules:
  0.0 72.2 jit_solution(13359819476286297009)
XLA Ops:
  0.0 1.9 %pack.1 = (bf16[256,512]{1,0:T(8,128)(2,1)S(1)}, bf16[128,1280]{1,0:T(8,128)(2,1)S(1)}, bf16[128,1280]{1,0:T(8,128)(2,1)S(1)}, bf16[128,1280]{1,0:T(8,128)(2,1)S(1)}, bf16[128,1280]{1,0:T(8,128)(2,1)S(1)}) custom-call(bf16[128,4096]{1,0:T(8,128)(2,1)} %tokens_ref.1, s32[128,256]{1,0:T(8,128)} %in_ref.1, s32[32,128]{1,0:T(8,128)} %bitcast.5, ...), custom_call_target="tpu_custom_call" | custom-call | flops 67108864 | bytes 3145728 | tf_op jit(solution)/shard_map/pack/pallas_call | solution.py:370
  1.9 4.1 %collective-permute-start = (bf16[256,512]{1,0:T(8,128)(2,1)S(1)}, bf16[256,512]{1,0:T(8,128)(2,1)S(1)}, u32[]{:S(2)}, u32[]{:S(2)}) collective-permute-start(bf16[256,512]{1,0:T(8,128)(2,1)S(1)} %get-tuple-element.31.refs_8_), channel_id=1, source_target_pairs={{0,16},{8,24},{16,0},{24,8},{1,17},{9,25},{17,1},{25,9},{2,18},{10... | collective-permute-start | bytes 786440 | tf_op jit(solution)/shard_map/ppermute | solution.py:353
  6.0 1.6 %collective-permute-start.5 = (bf16[256,512]{1,0:T(8,128)(2,1)S(1)}, bf16[256,512]{1,0:T(8,128)(2,1)S(1)}, u32[]{:S(2)}, u32[]{:S(2)}) collective-permute-start(bf16[256,512]{1,0:T(8,128)(2,1)S(1)} %get-tuple-element.31.refs_8_), channel_id=1, source_target_pairs={{0,8},{8,0},{16,24},{24,16},{1,9},{9,1},{17,25},{25,17},{2,10},{10... | collective-permute-start | bytes 786440 | tf_op jit(solution)/shard_map/ppermute | solution.py:353
  7.6 1.5 %collective-permute-start.2 = (bf16[128,1280]{1,0:T(8,128)(2,1)S(1)}, bf16[128,1280]{1,0:T(8,128)(2,1)S(1)}, u32[]{:S(2)}, u32[]{:S(2)}) collective-permute-start(bf16[128,1280]{1,0:T(8,128)(2,1)S(1)} %get-tuple-element.34), channel_id=1, source_target_pairs={{0,2},{2,0},{4,6},{6,4},{1,3},{3,1},{5,7},{7,5},{8,10},{10,8},{12,... | collective-permute-start | bytes 983048 | tf_op jit(solution)/shard_map/ppermute | solution.py:353
  9.1 1.5 %collective-permute-start.3 = (bf16[128,1280]{1,0:T(8,128)(2,1)S(1)}, bf16[128,1280]{1,0:T(8,128)(2,1)S(1)}, u32[]{:S(2)}, u32[]{:S(2)}) collective-permute-start(bf16[128,1280]{1,0:T(8,128)(2,1)S(1)} %get-tuple-element.35), channel_id=1, source_target_pairs={{0,4},{2,6},{4,0},{6,2},{1,5},{3,7},{5,1},{7,3},{8,12},{10,14},{12... | collective-permute-start | bytes 983048 | tf_op jit(solution)/shard_map/ppermute | solution.py:353
  11.1 7.0 %collective-permute-done.refs_10_ = bf16[256,512]{1,0:T(8,128)(2,1)S(1)} collective-permute-done((bf16[256,512]{1,0:T(8,128)(2,1)S(1)}, bf16[256,512]{1,0:T(8,128)(2,1)S(1)}, u32[]{:S(2)}, u32[]{:S(2)}) %collective-permute-start) | collective-permute-done | bytes 262176 | tf_op jit(solution)/shard_map/ppermute | solution.py:353
  18.7 3.2 %convolution_convert_fusion.gate_ref = bf16[128,512]{1,0:T(8,128)(2,1)S(1)} fusion(bf16[128,4096]{1,0:T(8,128)(2,1)} %tokens_ref.1, bf16[4096,512]{1,0:T(8,128)(2,1)} %param.14), kind=kOutput, calls=%fused_computation | convolution fusion | flops 536936448 | bytes 5373952 | tf_op jit(solution)/shard_map/dot_general | solution.py:413
  21.9 2.8 %collective-permute-done.3.refs_2_ = bf16[128,1280]{1,0:T(8,128)(2,1)S(1)} collective-permute-done((bf16[128,1280]{1,0:T(8,128)(2,1)S(1)}, bf16[128,1280]{1,0:T(8,128)(2,1)S(1)}, u32[]{:S(2)}, u32[]{:S(2)}) %collective-permute-start.3) | collective-permute-done | bytes 327712 | tf_op jit(solution)/shard_map/ppermute | solution.py:353
  24.7 0.8 %collective-permute-done.1.refs_11_ = bf16[256,512]{1,0:T(8,128)(2,1)S(1)} collective-permute-done((bf16[256,512]{1,0:T(8,128)(2,1)S(1)}, bf16[256,512]{1,0:T(8,128)(2,1)S(1)}, u32[]{:S(2)}, u32[]{:S(2)}) %collective-permute-start.1) | collective-permute-done | bytes 262176 | tf_op jit(solution)/shard_map/ppermute | solution.py:353
  26.0 1.1 %collective-permute-done.7.refs_5_ = bf16[128,1280]{1,0:T(8,128)(2,1)S(1)} collective-permute-done((bf16[128,1280]{1,0:T(8,128)(2,1)S(1)}, bf16[128,1280]{1,0:T(8,128)(2,1)S(1)}, u32[]{:S(2)}, u32[]{:S(2)}) %collective-permute-start.7) | collective-permute-done | bytes 327712 | tf_op jit(solution)/shard_map/ppermute | solution.py:353
  28.1 3.0 %project.1 = (bf16[64,1152]{1,0:T(8,128)(2,1)S(1)}, bf16[64,1152]{1,0:T(8,128)(2,1)S(1)}, bf16[64,1152]{1,0:T(8,128)(2,1)S(1)}, bf16[64,1152]{1,0:T(8,128)(2,1)S(1)}) custom-call(f32[128,512]{1,0:T(8,128)} %lags_ref.1, bf16[128,1280]{1,0:T(8,128)(2,1)S(1)} %get-tuple-element.39.refs_0_, bf16[128,1280]{1,0:T(8,128)(2,1)S(1)} %collective-permute-done.2.refs_1_, ...), custom_call_target="tpu_custom_call" | custom-call | flops 1073741824 | bytes 6291456 | tf_op jit(solution)/shard_map/project/pallas_call | solution.py:418
  31.0 1.3 %collective-permute-start.11 = (bf16[64,1152]{1,0:T(8,128)(2,1)S(1)}, bf16[64,1152]{1,0:T(8,128)(2,1)S(1)}, u32[]{:S(2)}, u32[]{:S(2)}) collective-permute-start(bf16[64,1152]{1,0:T(8,128)(2,1)S(1)} %get-tuple-element.48), channel_id=1, source_target_pairs={{0,2},{2,0},{4,6},{6,4},{1,3},{3,1},{5,7},{7,5},{8,10},{10,8},{12,... | collective-permute-start | bytes 442376 | tf_op jit(solution)/shard_map/ppermute | solution.py:353
  32.4 1.5 %collective-permute-start.12 = (bf16[64,1152]{1,0:T(8,128)(2,1)S(1)}, bf16[64,1152]{1,0:T(8,128)(2,1)S(1)}, u32[]{:S(2)}, u32[]{:S(2)}) collective-permute-start(bf16[64,1152]{1,0:T(8,128)(2,1)S(1)} %get-tuple-element.49), channel_id=1, source_target_pairs={{0,4},{2,6},{4,0},{6,2},{1,5},{3,7},{5,1},{7,3},{8,12},{10,14},{12... | collective-permute-start | bytes 442376 | tf_op jit(solution)/shard_map/ppermute | solution.py:353
  33.9 0.7 collective-permute-start.13
  34.6 3.2 %collective-permute-done.11.refs_1_ = bf16[64,1152]{1,0:T(8,128)(2,1)S(1)} collective-permute-done((bf16[64,1152]{1,0:T(8,128)(2,1)S(1)}, bf16[64,1152]{1,0:T(8,128)(2,1)S(1)}, u32[]{:S(2)}, u32[]{:S(2)}) %collective-permute-start.11) | collective-permute-done | bytes 147488 | tf_op jit(solution)/shard_map/ppermute | solution.py:353
  37.8 3.3 %collective-permute-done.12.refs_2_ = bf16[64,1152]{1,0:T(8,128)(2,1)S(1)} collective-permute-done((bf16[64,1152]{1,0:T(8,128)(2,1)S(1)}, bf16[64,1152]{1,0:T(8,128)(2,1)S(1)}, u32[]{:S(2)}, u32[]{:S(2)}) %collective-permute-start.12) | collective-permute-done | bytes 147488 | tf_op jit(solution)/shard_map/ppermute | solution.py:353
  41.3 1.7 %collective-permute-start.14 = (bf16[16,1536]{1,0:T(8,128)(2,1)S(1)}, bf16[16,1536]{1,0:T(8,128)(2,1)S(1)}, u32[]{:S(2)}, u32[]{:S(2)}) collective-permute-start(bf16[16,1536]{1,0:T(8,128)(2,1)S(1)} %get-tuple-element.54), channel_id=1, source_target_pairs={{0,8},{8,0},{16,24},{24,16},{1,9},{9,1},{17,25},{25,17},{2,10},{10... | collective-permute-start | bytes 147464 | tf_op jit(solution)/shard_map/ppermute | solution.py:353
  43.0 3.4 %collective-permute-start.15 = (bf16[16,1536]{1,0:T(8,128)(2,1)S(1)}, bf16[16,1536]{1,0:T(8,128)(2,1)S(1)}, u32[]{:S(2)}, u32[]{:S(2)}) collective-permute-start(bf16[16,1536]{1,0:T(8,128)(2,1)S(1)} %get-tuple-element.55), channel_id=1, source_target_pairs={{0,16},{8,24},{16,0},{24,8},{1,17},{9,25},{17,1},{25,9},{2,18},{10... | collective-permute-start | bytes 147464 | tf_op jit(solution)/shard_map/ppermute | solution.py:353
  46.4 3.1 %collective-permute-start.10 = (bf16[2,512]{1,0:T(2,128)(2,1)S(1)}, bf16[2,512]{1,0:T(2,128)(2,1)S(1)}, u32[]{:S(2)}, u32[]{:S(2)}) collective-permute-start(bf16[2,512]{1,0:T(2,128)(2,1)S(1)} %slice.3), channel_id=1, source_target_pairs={{0,2},{2,4},{4,6},{6,8},{8,10},{10,12},{12,14},{14,16},{16,18},{18... | collective-permute-start | bytes 6152 | tf_op jit(solution)/shard_map/ppermute | solution.py:434
  49.5 1.3 %collective-permute-done.10.before_ref = bf16[2,512]{1,0:T(2,128)(2,1)S(1)} collective-permute-done((bf16[2,512]{1,0:T(2,128)(2,1)S(1)}, bf16[2,512]{1,0:T(2,128)(2,1)S(1)}, u32[]{:S(2)}, u32[]{:S(2)}) %collective-permute-start.10) | collective-permute-done | bytes 2080 | tf_op jit(solution)/shard_map/ppermute | solution.py:434
  50.8 1.5 %collective-permute-done.16.refs_3_ = bf16[16,1536]{1,0:T(8,128)(2,1)S(1)} collective-permute-done((bf16[16,1536]{1,0:T(8,128)(2,1)S(1)}, bf16[16,1536]{1,0:T(8,128)(2,1)S(1)}, u32[]{:S(2)}, u32[]{:S(2)}) %collective-permute-start.16) | collective-permute-done | bytes 49184 | tf_op jit(solution)/shard_map/ppermute | solution.py:353
  52.3 2.5 %mix.1 = bf16[32,16,128]{2,1,0:T(8,128)(2,1)S(1)} custom-call(f32[3,1024]{1,0:T(4,128)S(1)} %copy-done, bf16[16,1536]{1,0:T(8,128)(2,1)S(1)} %get-tuple-element.53.refs_0_, bf16[16,1536]{1,0:T(8,128)(2,1)S(1)} %collective-permute-done.14.refs_1_, bf16[16,1536]{1,0:T(8,128)(2,1)S(1)} %collective-permute-done.15.refs_2_, ...), custom_call_target="tpu_custom_call" | custom-call | flops 536870912 | bytes 2097152 | tf_op jit(solution)/shard_map/mix/pallas_call | solution.py:459
  54.8 13.4 %all_to_all.5 = bf16[32,16,128]{2,1,0:T(8,128)(2,1)S(1)} all-to-all(bf16[32,16,128]{2,1,0:T(8,128)(2,1)S(1)} %mix.1), channel_id=1, replica_groups=mesh['far'=4,'near'=4,'dp'=2] {'dp','far','near'}, dimensions={0} | all-to-all | bytes 262144 | tf_op jit(solution)/shard_map/all_to_all | solution.py:476
  68.2 4.1 %project_out.1 = bf16[128,4096]{1,0:T(8,128)(2,1)} custom-call(bf16[128,512]{1,0:T(8,128)(2,1)S(1)} %convolution_convert_fusion.gate_ref, bf16[2,512]{1,0:T(2,128)(2,1)S(1)} %collective-permute-done.10.before_ref, f32[3,1024]{1,0:T(4,128)S(1)} %copy-done, bf16[512,128]{1,0:T(8,128)(2,1)S(1)} %bitcast.4, bf16[512,4096]{1,0:T(8,128)(2,1)} %source_ref.1), custom_call_target="tpu_custom_call" | custom-call | flops 536870912 | bytes 5242880 | tf_op jit(solution)/shard_map/project_out/pallas_call | solution.py:478
  (20 shorter events, 2.7 us)
Async XLA Ops:
  1.9 16.1 %collective-permute-start = (bf16[256,512]{1,0:T(8,128)(2,1)S(1)}, bf16[256,512]{1,0:T(8,128)(2,1)S(1)}, u32[]{:S(2)}, u32[]{:S(2)}) collective-permute-start(bf16[256,512]{1,0:T(8,128)(2,1)S(1)} %get-tuple-element.31.refs_8_), channel_id=1, source_target_pairs={{0,16},{8,24},{16,0},{24,8},{1,17},{9,25},{17,1},{25,9},{2,18},{10... | collective-permute-start | bytes 786440 | tf_op jit(solution)/shard_map/ppermute | solution.py:353
  6.0 12.6 %collective-permute-start.5 = (bf16[256,512]{1,0:T(8,128)(2,1)S(1)}, bf16[256,512]{1,0:T(8,128)(2,1)S(1)}, u32[]{:S(2)}, u32[]{:S(2)}) collective-permute-start(bf16[256,512]{1,0:T(8,128)(2,1)S(1)} %get-tuple-element.31.refs_8_), channel_id=1, source_target_pairs={{0,8},{8,0},{16,24},{24,16},{1,9},{9,1},{17,25},{25,17},{2,10},{10... | collective-permute-start | bytes 786440 | tf_op jit(solution)/shard_map/ppermute | solution.py:353
  7.6 14.3 %collective-permute-start.2 = (bf16[128,1280]{1,0:T(8,128)(2,1)S(1)}, bf16[128,1280]{1,0:T(8,128)(2,1)S(1)}, u32[]{:S(2)}, u32[]{:S(2)}) collective-permute-start(bf16[128,1280]{1,0:T(8,128)(2,1)S(1)} %get-tuple-element.34), channel_id=1, source_target_pairs={{0,2},{2,0},{4,6},{6,4},{1,3},{3,1},{5,7},{7,5},{8,10},{10,8},{12,... | collective-permute-start | bytes 983048 | tf_op jit(solution)/shard_map/ppermute | solution.py:353
  9.1 15.6 %collective-permute-start.3 = (bf16[128,1280]{1,0:T(8,128)(2,1)S(1)}, bf16[128,1280]{1,0:T(8,128)(2,1)S(1)}, u32[]{:S(2)}, u32[]{:S(2)}) collective-permute-start(bf16[128,1280]{1,0:T(8,128)(2,1)S(1)} %get-tuple-element.35), channel_id=1, source_target_pairs={{0,4},{2,6},{4,0},{6,2},{1,5},{3,7},{5,1},{7,3},{8,12},{10,14},{12... | collective-permute-start | bytes 983048 | tf_op jit(solution)/shard_map/ppermute | solution.py:353
  10.6 14.1 %collective-permute-start.4 = (bf16[128,1280]{1,0:T(8,128)(2,1)S(1)}, bf16[128,1280]{1,0:T(8,128)(2,1)S(1)}, u32[]{:S(2)}, u32[]{:S(2)}) collective-permute-start(bf16[128,1280]{1,0:T(8,128)(2,1)S(1)} %get-tuple-element.36), channel_id=1, source_target_pairs={{0,6},{2,4},{4,2},{6,0},{1,7},{3,5},{5,3},{7,1},{8,14},{10,12},{12... | collective-permute-start | bytes 983048 | tf_op jit(solution)/shard_map/ppermute | solution.py:353
  18.1 7.4 %collective-permute-start.1 = (bf16[256,512]{1,0:T(8,128)(2,1)S(1)}, bf16[256,512]{1,0:T(8,128)(2,1)S(1)}, u32[]{:S(2)}, u32[]{:S(2)}) collective-permute-start(bf16[256,512]{1,0:T(8,128)(2,1)S(1)} %collective-permute-done.refs_10_), channel_id=1, source_target_pairs={{0,8},{8,0},{16,24},{24,16},{1,9},{9,1},{17,25},{25,17},{2,10},{10... | collective-permute-start | bytes 786440 | tf_op jit(solution)/shard_map/ppermute | solution.py:353
  18.7 33.6 %copy-start = (f32[3,1024]{1,0:T(4,128)S(1)}, f32[3,1024]{1,0:T(4,128)}, u32[]{:S(2)}) copy-start(f32[3,1024]{1,0:T(4,128)} %taps_ref.3) | copy-start | bytes 36868
  18.7 7.3 %collective-permute-start.6 = (bf16[128,1280]{1,0:T(8,128)(2,1)S(1)}, bf16[128,1280]{1,0:T(8,128)(2,1)S(1)}, u32[]{:S(2)}, u32[]{:S(2)}) collective-permute-start(bf16[128,1280]{1,0:T(8,128)(2,1)S(1)} %get-tuple-element.39.refs_0_), channel_id=1, source_target_pairs={{0,1},{1,0},{2,3},{3,2},{4,5},{5,4},{6,7},{7,6},{8,9},{9,8},{10,11... | collective-permute-start | bytes 983048 | tf_op jit(solution)/shard_map/ppermute | solution.py:353
  25.5 1.6 %collective-permute-start.7 = (bf16[128,1280]{1,0:T(8,128)(2,1)S(1)}, bf16[128,1280]{1,0:T(8,128)(2,1)S(1)}, u32[]{:S(2)}, u32[]{:S(2)}) collective-permute-start(bf16[128,1280]{1,0:T(8,128)(2,1)S(1)} %collective-permute-done.2.refs_1_), channel_id=1, source_target_pairs={{0,1},{1,0},{2,3},{3,2},{4,5},{5,4},{6,7},{7,6},{8,9},{9,8},{10,11... | collective-permute-start | bytes 983048 | tf_op jit(solution)/shard_map/ppermute | solution.py:353
  25.5 2.1 %collective-permute-start.8 = (bf16[128,1280]{1,0:T(8,128)(2,1)S(1)}, bf16[128,1280]{1,0:T(8,128)(2,1)S(1)}, u32[]{:S(2)}, u32[]{:S(2)}) collective-permute-start(bf16[128,1280]{1,0:T(8,128)(2,1)S(1)} %collective-permute-done.3.refs_2_), channel_id=1, source_target_pairs={{0,1},{1,0},{2,3},{3,2},{4,5},{5,4},{6,7},{7,6},{8,9},{9,8},{10,11... | collective-permute-start | bytes 983048 | tf_op jit(solution)/shard_map/ppermute | solution.py:353
  26.0 2.1 %collective-permute-start.9 = (bf16[128,1280]{1,0:T(8,128)(2,1)S(1)}, bf16[128,1280]{1,0:T(8,128)(2,1)S(1)}, u32[]{:S(2)}, u32[]{:S(2)}) collective-permute-start(bf16[128,1280]{1,0:T(8,128)(2,1)S(1)} %collective-permute-done.4.refs_3_), channel_id=1, source_target_pairs={{0,1},{1,0},{2,3},{3,2},{4,5},{5,4},{6,7},{7,6},{8,9},{9,8},{10,11... | collective-permute-start | bytes 983048 | tf_op jit(solution)/shard_map/ppermute | solution.py:353
  31.0 6.8 %collective-permute-start.11 = (bf16[64,1152]{1,0:T(8,128)(2,1)S(1)}, bf16[64,1152]{1,0:T(8,128)(2,1)S(1)}, u32[]{:S(2)}, u32[]{:S(2)}) collective-permute-start(bf16[64,1152]{1,0:T(8,128)(2,1)S(1)} %get-tuple-element.48), channel_id=1, source_target_pairs={{0,2},{2,0},{4,6},{6,4},{1,3},{3,1},{5,7},{7,5},{8,10},{10,8},{12,... | collective-permute-start | bytes 442376 | tf_op jit(solution)/shard_map/ppermute | solution.py:353
  32.4 8.8 %collective-permute-start.12 = (bf16[64,1152]{1,0:T(8,128)(2,1)S(1)}, bf16[64,1152]{1,0:T(8,128)(2,1)S(1)}, u32[]{:S(2)}, u32[]{:S(2)}) collective-permute-start(bf16[64,1152]{1,0:T(8,128)(2,1)S(1)} %get-tuple-element.49), channel_id=1, source_target_pairs={{0,4},{2,6},{4,0},{6,2},{1,5},{3,7},{5,1},{7,3},{8,12},{10,14},{12... | collective-permute-start | bytes 442376 | tf_op jit(solution)/shard_map/ppermute | solution.py:353
  33.9 7.2 %collective-permute-start.13 = (bf16[64,1152]{1,0:T(8,128)(2,1)S(1)}, bf16[64,1152]{1,0:T(8,128)(2,1)S(1)}, u32[]{:S(2)}, u32[]{:S(2)}) collective-permute-start(bf16[64,1152]{1,0:T(8,128)(2,1)S(1)} %get-tuple-element.50), channel_id=1, source_target_pairs={{0,6},{2,4},{4,2},{6,0},{1,7},{3,5},{5,3},{7,1},{8,14},{10,12},{12... | collective-permute-start | bytes 442376 | tf_op jit(solution)/shard_map/ppermute | solution.py:353
  41.3 9.5 %collective-permute-start.14 = (bf16[16,1536]{1,0:T(8,128)(2,1)S(1)}, bf16[16,1536]{1,0:T(8,128)(2,1)S(1)}, u32[]{:S(2)}, u32[]{:S(2)}) collective-permute-start(bf16[16,1536]{1,0:T(8,128)(2,1)S(1)} %get-tuple-element.54), channel_id=1, source_target_pairs={{0,8},{8,0},{16,24},{24,16},{1,9},{9,1},{17,25},{25,17},{2,10},{10... | collective-permute-start | bytes 147464 | tf_op jit(solution)/shard_map/ppermute | solution.py:353
  43.0 7.8 %collective-permute-start.15 = (bf16[16,1536]{1,0:T(8,128)(2,1)S(1)}, bf16[16,1536]{1,0:T(8,128)(2,1)S(1)}, u32[]{:S(2)}, u32[]{:S(2)}) collective-permute-start(bf16[16,1536]{1,0:T(8,128)(2,1)S(1)} %get-tuple-element.55), channel_id=1, source_target_pairs={{0,16},{8,24},{16,0},{24,8},{1,17},{9,25},{17,1},{25,9},{2,18},{10... | collective-permute-start | bytes 147464 | tf_op jit(solution)/shard_map/ppermute | solution.py:353
  46.4 5.9 %collective-permute-start.16 = (bf16[16,1536]{1,0:T(8,128)(2,1)S(1)}, bf16[16,1536]{1,0:T(8,128)(2,1)S(1)}, u32[]{:S(2)}, u32[]{:S(2)}) collective-permute-start(bf16[16,1536]{1,0:T(8,128)(2,1)S(1)} %get-tuple-element.56), channel_id=1, source_target_pairs={{0,24},{8,16},{16,8},{24,0},{1,25},{9,17},{17,9},{25,1},{2,26},{10... | collective-permute-start | bytes 147464 | tf_op jit(solution)/shard_map/ppermute | solution.py:353
  46.4 4.4 %collective-permute-start.10 = (bf16[2,512]{1,0:T(2,128)(2,1)S(1)}, bf16[2,512]{1,0:T(2,128)(2,1)S(1)}, u32[]{:S(2)}, u32[]{:S(2)}) collective-permute-start(bf16[2,512]{1,0:T(2,128)(2,1)S(1)} %slice.3), channel_id=1, source_target_pairs={{0,2},{2,4},{4,6},{6,8},{8,10},{10,12},{12,14},{14,16},{16,18},{18... | collective-permute-start | bytes 6152 | tf_op jit(solution)/shard_map/ppermute | solution.py:434
where the time goes:
time: 72.4 us; the launch traced here: 72.2 us
  starting transfers between devices  22.1 us (31%)
  waiting for transfers between devices  21.8 us (30%)
  blocking collectives  13.4 us (19%)
  Pallas kernels  11.6 us (16%)
  matrix products  3.23 us (4%)
    ppermute x16, waiting for transfers between devices, exchanged(): lax.ppermute(value, axis, [(i, i ^ step) for i in range(lax.axis_size(axi...  20.6 us
    ppermute x16, starting transfers between devices, exchanged(): lax.ppermute(value, axis, [(i, i ^ step) for i in range(lax.axis_size(axi...  19 us
    all_to_all x1, blocking collectives, on_device(): lax.all_to_all(mixed, ('dp', 'far', 'near'), 0, 0, tiled=True)  13.4 us
    pallas_call x1, Pallas kernels, on_device(): pl.pallas_call(out_kernel, in_specs=[ANY] * 4 + [HBM], out_specs=HBM, out...  4.08 us
    dot_general x1, matrix products, on_device(): jnp.dot(late_tokens, w_gate, preferred_element_type=F32).astype(BF16)  3.23 us
    ppermute x1, starting transfers between devices, on_device(): lax.ppermute(last_rows, ('far', 'near'), [(i, i + 1) for i in range(count...  3.13 us
    pallas_call x1, Pallas kernels, on_device(): pl.pallas_call(functools.partial(project_kernel, near, far, cores, depth)...  2.97 us
    pallas_call x1, Pallas kernels, on_device(): pl.pallas_call(functools.partial(mix_kernel, near, far, cores, held), in_...  2.52 us
  transfers between devices with their start and end apart: 17, of which 10 were waited for; matrix products, arithmetic and copies ran while one was open for 4% of the time, Pallas kernels for 0%

commit v1 on v0

--- a/solution.py
+++ b/solution.py
@@ -411,7 +411,8 @@
         late_tokens, pieces[2] = lax.optimization_barrier((tokens, pieces[2]))
         pieces[3] = exchanged(pieces[2], "far", 1)
     gate_rows = jnp.dot(late_tokens, w_gate, preferred_element_type=F32).astype(BF16)
-    gate_rows, pieces[-1], *chunks[1:] = lax.optimization_barrier((gate_rows, pieces[-1], *chunks[1:]))
+    gate_rows, *chunks[1:] = lax.optimization_barrier((gate_rows, *chunks[1:]))
+    pieces[-1], chunks[-1] = lax.optimization_barrier((pieces[-1], chunks[-1]))
     chunks += [exchanged(chunk, "dp", 1) for chunk in chunks]
 
     near_shape = jax.ShapeDtypeStruct((far * held, (cores * near + 1) * rows), BF16)
@@ -433,6 +434,7 @@
     last_rows, partial[0] = lax.optimization_barrier((gate_rows[rows - 2 :], partial[0]))
     before = lax.ppermute(last_rows, ("far", "near"), [(i, i + 1) for i in range(count - 1)])
     partial = [partial[0]] + [exchanged(partial[step], "near", step) for step in range(1, near)]
+    before, *partial = lax.optimization_barrier((before, *partial))
 
     far_shape = (held, (cores + 1) * near * rows)
     parts = pl.pallas_call(
@@ -451,7 +453,6 @@
         order = jnp.arange(far) ^ lax.axis_index("far")
         parts = lax.all_to_all(jnp.take(jnp.stack(parts), order, axis=0), "far", 0, 0, tiled=True)
         parts = [parts.reshape(far * held, far_shape[1])]
-    before, parts[0] = lax.optimization_barrier((before, parts[0]))
 
     tiles = length // LANES
     all_rows = tiles * SLOTS * cores * GROUP

time: 72.4 us -> 68.3 us (0.943)
  blocking collectives: 13.4 us -> 9.62 us
    all_to_all x1, blocking collectives: 13.4 us -> 9.62 us  [on_device(): lax.all_to_all(mixed, ('dp', 'far', 'near'), 0, 0, tiled=True)]
    ppermute x16, waiting for transfers between devices: 20.6 us -> 19.8 us  [exchanged(): lax.ppermute(value, axis, [(i, i ^ step) for i in range(lax.axis_size(axi...]
  transfers between devices with their start and end apart: 17 -> 17, of which waited for: 10 -> 11; matrix products, arithmetic and copies ran while one was open for 4% -> 5% of each run, Pallas kernels for 0% -> 0%
where the time goes in v1:
time: 68.3 us; the launch traced here: 68.1 us
  starting transfers between devices  22.4 us (33%)
  waiting for transfers between devices  21.1 us (31%)
  Pallas kernels  11.6 us (17%)
  blocking collectives  9.62 us (14%)
  matrix products  3.23 us (5%)
    ppermute x16, waiting for transfers between devices, exchanged(): lax.ppermute(value, axis, [(i, i ^ step) for i in range(lax.axis_size(axi...  19.8 us
    ppermute x16, starting transfers between devices, exchanged(): lax.ppermute(value, axis, [(i, i ^ step) for i in range(lax.axis_size(axi...  19.3 us
    all_to_all x1, blocking collectives, on_device(): lax.all_to_all(mixed, ('dp', 'far', 'near'), 0, 0, tiled=True)  9.62 us
    pallas_call x1, Pallas kernels, on_device(): pl.pallas_call(out_kernel, in_specs=[ANY] * 4 + [HBM], out_specs=HBM, out...  4.09 us
    dot_general x1, matrix products, on_device(): jnp.dot(late_tokens, w_gate, preferred_element_type=F32).astype(BF16)  3.23 us
    ppermute x1, starting transfers between devices, on_device(): lax.ppermute(last_rows, ('far', 'near'), [(i, i + 1) for i in range(count...  3.13 us
    pallas_call x1, Pallas kernels, on_device(): pl.pallas_call(functools.partial(project_kernel, near, far, cores, depth)...  2.97 us
    pallas_call x1, Pallas kernels, on_device(): pl.pallas_call(functools.partial(mix_kernel, near, far, cores, held), in_...  2.52 us
  transfers between devices with their start and end apart: 17, of which 11 were waited for; matrix products, arithmetic and copies ran while one was open for 5% of the time, Pallas kernels for 0%

profile of v1, /device:TPU:0, one launch (start us, length us, event | category | flops | bytes accessed | tf_op | source)
XLA Modules:
  0.0 68.1 jit_solution(13336446500247880440)
XLA Ops:
  0.0 1.9 %pack.1 = (bf16[256,512]{1,0:T(8,128)(2,1)S(1)}, bf16[128,1280]{1,0:T(8,128)(2,1)S(1)}, bf16[128,1280]{1,0:T(8,128)(2,1)S(1)}, bf16[128,1280]{1,0:T(8,128)(2,1)S(1)}, bf16[128,1280]{1,0:T(8,128)(2,1)S(1)}) custom-call(bf16[128,4096]{1,0:T(8,128)(2,1)} %tokens_ref.1, s32[128,256]{1,0:T(8,128)} %in_ref.1, s32[32,128]{1,0:T(8,128)} %bitcast.5, ...), custom_call_target="tpu_custom_call" | custom-call | flops 67108864 | bytes 3145728 | tf_op jit(solution)/shard_map/pack/pallas_call | solution.py:370
  1.9 4.1 %collective-permute-start = (bf16[256,512]{1,0:T(8,128)(2,1)S(1)}, bf16[256,512]{1,0:T(8,128)(2,1)S(1)}, u32[]{:S(2)}, u32[]{:S(2)}) collective-permute-start(bf16[256,512]{1,0:T(8,128)(2,1)S(1)} %get-tuple-element.35.refs_8_), channel_id=1, source_target_pairs={{0,16},{8,24},{16,0},{24,8},{1,17},{9,25},{17,1},{25,9},{2,18},{10... | collective-permute-start | bytes 786440 | tf_op jit(solution)/shard_map/ppermute | solution.py:353
  6.0 1.6 %collective-permute-start.4 = (bf16[256,512]{1,0:T(8,128)(2,1)S(1)}, bf16[256,512]{1,0:T(8,128)(2,1)S(1)}, u32[]{:S(2)}, u32[]{:S(2)}) collective-permute-start(bf16[256,512]{1,0:T(8,128)(2,1)S(1)} %get-tuple-element.35.refs_8_), channel_id=1, source_target_pairs={{0,8},{8,0},{16,24},{24,16},{1,9},{9,1},{17,25},{25,17},{2,10},{10... | collective-permute-start | bytes 786440 | tf_op jit(solution)/shard_map/ppermute | solution.py:353
  7.6 1.5 %collective-permute-start.1 = (bf16[128,1280]{1,0:T(8,128)(2,1)S(1)}, bf16[128,1280]{1,0:T(8,128)(2,1)S(1)}, u32[]{:S(2)}, u32[]{:S(2)}) collective-permute-start(bf16[128,1280]{1,0:T(8,128)(2,1)S(1)} %get-tuple-element.37), channel_id=1, source_target_pairs={{0,2},{2,0},{4,6},{6,4},{1,3},{3,1},{5,7},{7,5},{8,10},{10,8},{12,... | collective-permute-start | bytes 983048 | tf_op jit(solution)/shard_map/ppermute | solution.py:353
  9.1 1.5 %collective-permute-start.2 = (bf16[128,1280]{1,0:T(8,128)(2,1)S(1)}, bf16[128,1280]{1,0:T(8,128)(2,1)S(1)}, u32[]{:S(2)}, u32[]{:S(2)}) collective-permute-start(bf16[128,1280]{1,0:T(8,128)(2,1)S(1)} %get-tuple-element.38), channel_id=1, source_target_pairs={{0,4},{2,6},{4,0},{6,2},{1,5},{3,7},{5,1},{7,3},{8,12},{10,14},{12... | collective-permute-start | bytes 983048 | tf_op jit(solution)/shard_map/ppermute | solution.py:353
  11.1 7.0 %collective-permute-done.refs_10_ = bf16[256,512]{1,0:T(8,128)(2,1)S(1)} collective-permute-done((bf16[256,512]{1,0:T(8,128)(2,1)S(1)}, bf16[256,512]{1,0:T(8,128)(2,1)S(1)}, u32[]{:S(2)}, u32[]{:S(2)}) %collective-permute-start) | collective-permute-done | bytes 262176 | tf_op jit(solution)/shard_map/ppermute | solution.py:353
  18.7 3.2 %convolution_convert_fusion.gate_ref = bf16[128,512]{1,0:T(8,128)(2,1)S(1)} fusion(bf16[128,4096]{1,0:T(8,128)(2,1)} %tokens_ref.1, bf16[4096,512]{1,0:T(8,128)(2,1)} %param.14), kind=kOutput, calls=%fused_computation | convolution fusion | flops 536936448 | bytes 5373952 | tf_op jit(solution)/shard_map/dot_general | solution.py:413
  21.9 2.8 %collective-permute-done.2.refs_2_ = bf16[128,1280]{1,0:T(8,128)(2,1)S(1)} collective-permute-done((bf16[128,1280]{1,0:T(8,128)(2,1)S(1)}, bf16[128,1280]{1,0:T(8,128)(2,1)S(1)}, u32[]{:S(2)}, u32[]{:S(2)}) %collective-permute-start.2) | collective-permute-done | bytes 327712 | tf_op jit(solution)/shard_map/ppermute | solution.py:353
  25.5 0.9 %collective-permute-done.7.refs_5_ = bf16[128,1280]{1,0:T(8,128)(2,1)S(1)} collective-permute-done((bf16[128,1280]{1,0:T(8,128)(2,1)S(1)}, bf16[128,1280]{1,0:T(8,128)(2,1)S(1)}, u32[]{:S(2)}, u32[]{:S(2)}) %collective-permute-start.7) | collective-permute-done | bytes 327712 | tf_op jit(solution)/shard_map/ppermute | solution.py:353
  27.3 3.0 %project.1 = (bf16[64,1152]{1,0:T(8,128)(2,1)S(1)}, bf16[64,1152]{1,0:T(8,128)(2,1)S(1)}, bf16[64,1152]{1,0:T(8,128)(2,1)S(1)}, bf16[64,1152]{1,0:T(8,128)(2,1)S(1)}) custom-call(f32[128,512]{1,0:T(8,128)} %lags_ref.1, bf16[128,1280]{1,0:T(8,128)(2,1)S(1)} %get-tuple-element.42.refs_0_, bf16[128,1280]{1,0:T(8,128)(2,1)S(1)} %collective-permute-done.1.refs_1_, ...), custom_call_target="tpu_custom_call" | custom-call | flops 1073741824 | bytes 6291456 | tf_op jit(solution)/shard_map/project/pallas_call | solution.py:419
  30.3 1.3 %collective-permute-start.11 = (bf16[64,1152]{1,0:T(8,128)(2,1)S(1)}, bf16[64,1152]{1,0:T(8,128)(2,1)S(1)}, u32[]{:S(2)}, u32[]{:S(2)}) collective-permute-start(bf16[64,1152]{1,0:T(8,128)(2,1)S(1)} %get-tuple-element.53), channel_id=1, source_target_pairs={{0,2},{2,0},{4,6},{6,4},{1,3},{3,1},{5,7},{7,5},{8,10},{10,8},{12,... | collective-permute-start | bytes 442376 | tf_op jit(solution)/shard_map/ppermute | solution.py:353
  31.6 1.4 %collective-permute-start.12 = (bf16[64,1152]{1,0:T(8,128)(2,1)S(1)}, bf16[64,1152]{1,0:T(8,128)(2,1)S(1)}, u32[]{:S(2)}, u32[]{:S(2)}) collective-permute-start(bf16[64,1152]{1,0:T(8,128)(2,1)S(1)} %get-tuple-element.54), channel_id=1, source_target_pairs={{0,4},{2,6},{4,0},{6,2},{1,5},{3,7},{5,1},{7,3},{8,12},{10,14},{12... | collective-permute-start | bytes 442376 | tf_op jit(solution)/shard_map/ppermute | solution.py:353
  33.0 0.9 %collective-permute-start.13 = (bf16[64,1152]{1,0:T(8,128)(2,1)S(1)}, bf16[64,1152]{1,0:T(8,128)(2,1)S(1)}, u32[]{:S(2)}, u32[]{:S(2)}) collective-permute-start(bf16[64,1152]{1,0:T(8,128)(2,1)S(1)} %get-tuple-element.55), channel_id=1, source_target_pairs={{0,6},{2,4},{4,2},{6,0},{1,7},{3,5},{5,3},{7,1},{8,14},{10,12},{12... | collective-permute-start | bytes 442376 | tf_op jit(solution)/shard_map/ppermute | solution.py:353
  33.9 3.1 %collective-permute-start.10 = (bf16[2,512]{1,0:T(2,128)(2,1)S(1)}, bf16[2,512]{1,0:T(2,128)(2,1)S(1)}, u32[]{:S(2)}, u32[]{:S(2)}) collective-permute-start(bf16[2,512]{1,0:T(2,128)(2,1)S(1)} %slice.3), channel_id=1, source_target_pairs={{0,2},{2,4},{4,6},{6,8},{8,10},{10,12},{12,14},{14,16},{16,18},{18... | collective-permute-start | bytes 6152 | tf_op jit(solution)/shard_map/ppermute | solution.py:435
  37.0 1.3 %collective-permute-done.10.before_ref = bf16[2,512]{1,0:T(2,128)(2,1)S(1)} collective-permute-done((bf16[2,512]{1,0:T(2,128)(2,1)S(1)}, bf16[2,512]{1,0:T(2,128)(2,1)S(1)}, u32[]{:S(2)}, u32[]{:S(2)}) %collective-permute-start.10) | collective-permute-done | bytes 2080 | tf_op jit(solution)/shard_map/ppermute | solution.py:435
  38.3 1.0 %collective-permute-done.12.refs_2_ = bf16[64,1152]{1,0:T(8,128)(2,1)S(1)} collective-permute-done((bf16[64,1152]{1,0:T(8,128)(2,1)S(1)}, bf16[64,1152]{1,0:T(8,128)(2,1)S(1)}, u32[]{:S(2)}, u32[]{:S(2)}) %collective-permute-start.12) | collective-permute-done | bytes 147488 | tf_op jit(solution)/shard_map/ppermute | solution.py:353
  39.3 1.1 %collective-permute-done.13.refs_3_ = bf16[64,1152]{1,0:T(8,128)(2,1)S(1)} collective-permute-done((bf16[64,1152]{1,0:T(8,128)(2,1)S(1)}, bf16[64,1152]{1,0:T(8,128)(2,1)S(1)}, u32[]{:S(2)}, u32[]{:S(2)}) %collective-permute-start.13) | collective-permute-done | bytes 147488 | tf_op jit(solution)/shard_map/ppermute | solution.py:353
  40.5 2.1 %collective-permute-start.14 = (bf16[16,1536]{1,0:T(8,128)(2,1)S(1)}, bf16[16,1536]{1,0:T(8,128)(2,1)S(1)}, u32[]{:S(2)}, u32[]{:S(2)}) collective-permute-start(bf16[16,1536]{1,0:T(8,128)(2,1)S(1)} %get-tuple-element.62), channel_id=1, source_target_pairs={{0,8},{8,0},{16,24},{24,16},{1,9},{9,1},{17,25},{25,17},{2,10},{10... | collective-permute-start | bytes 147464 | tf_op jit(solution)/shard_map/ppermute | solution.py:353
  42.6 3.4 %collective-permute-start.15 = (bf16[16,1536]{1,0:T(8,128)(2,1)S(1)}, bf16[16,1536]{1,0:T(8,128)(2,1)S(1)}, u32[]{:S(2)}, u32[]{:S(2)}) collective-permute-start(bf16[16,1536]{1,0:T(8,128)(2,1)S(1)} %get-tuple-element.63), channel_id=1, source_target_pairs={{0,16},{8,24},{16,0},{24,8},{1,17},{9,25},{17,1},{25,9},{2,18},{10... | collective-permute-start | bytes 147464 | tf_op jit(solution)/shard_map/ppermute | solution.py:353
  46.0 3.1 %collective-permute-done.15.refs_2_ = bf16[16,1536]{1,0:T(8,128)(2,1)S(1)} collective-permute-done((bf16[16,1536]{1,0:T(8,128)(2,1)S(1)}, bf16[16,1536]{1,0:T(8,128)(2,1)S(1)}, u32[]{:S(2)}, u32[]{:S(2)}) %collective-permute-start.15) | collective-permute-done | bytes 49184 | tf_op jit(solution)/shard_map/ppermute | solution.py:353
  49.1 2.8 %collective-permute-done.16.refs_3_ = bf16[16,1536]{1,0:T(8,128)(2,1)S(1)} collective-permute-done((bf16[16,1536]{1,0:T(8,128)(2,1)S(1)}, bf16[16,1536]{1,0:T(8,128)(2,1)S(1)}, u32[]{:S(2)}, u32[]{:S(2)}) %collective-permute-start.16) | collective-permute-done | bytes 49184 | tf_op jit(solution)/shard_map/ppermute | solution.py:353
  51.8 2.5 %mix.1 = bf16[32,16,128]{2,1,0:T(8,128)(2,1)S(1)} custom-call(f32[3,1024]{1,0:T(4,128)S(1)} %copy-done, bf16[16,1536]{1,0:T(8,128)(2,1)S(1)} %get-tuple-element.61.refs_0_, bf16[16,1536]{1,0:T(8,128)(2,1)S(1)} %collective-permute-done.14.refs_1_, bf16[16,1536]{1,0:T(8,128)(2,1)S(1)} %collective-permute-done.15.refs_2_, ...), custom_call_target="tpu_custom_call" | custom-call | flops 536870912 | bytes 2097152 | tf_op jit(solution)/shard_map/mix/pallas_call | solution.py:460
  54.4 9.6 %all_to_all.5 = bf16[32,16,128]{2,1,0:T(8,128)(2,1)S(1)} all-to-all(bf16[32,16,128]{2,1,0:T(8,128)(2,1)S(1)} %mix.1), channel_id=1, replica_groups=mesh['far'=4,'near'=4,'dp'=2] {'dp','far','near'}, dimensions={0} | all-to-all | bytes 262144 | tf_op jit(solution)/shard_map/all_to_all | solution.py:477
  64.0 4.1 %project_out.1 = bf16[128,4096]{1,0:T(8,128)(2,1)} custom-call(bf16[128,512]{1,0:T(8,128)(2,1)S(1)} %convolution_convert_fusion.gate_ref, bf16[2,512]{1,0:T(2,128)(2,1)S(1)} %collective-permute-done.10.before_ref, f32[3,1024]{1,0:T(4,128)S(1)} %copy-done, bf16[512,128]{1,0:T(8,128)(2,1)S(1)} %bitcast.4, bf16[512,4096]{1,0:T(8,128)(2,1)} %source_ref.1), custom_call_target="tpu_custom_call" | custom-call | flops 536870912 | bytes 5242880 | tf_op jit(solution)/shard_map/project_out/pallas_call | solution.py:479
  (20 shorter events, 2.9 us)
Async XLA Ops:
  1.9 16.1 %collective-permute-start = (bf16[256,512]{1,0:T(8,128)(2,1)S(1)}, bf16[256,512]{1,0:T(8,128)(2,1)S(1)}, u32[]{:S(2)}, u32[]{:S(2)}) collective-permute-start(bf16[256,512]{1,0:T(8,128)(2,1)S(1)} %get-tuple-element.35.refs_8_), channel_id=1, source_target_pairs={{0,16},{8,24},{16,0},{24,8},{1,17},{9,25},{17,1},{25,9},{2,18},{10... | collective-permute-start | bytes 786440 | tf_op jit(solution)/shard_map/ppermute | solution.py:353
  6.0 12.6 %collective-permute-start.4 = (bf16[256,512]{1,0:T(8,128)(2,1)S(1)}, bf16[256,512]{1,0:T(8,128)(2,1)S(1)}, u32[]{:S(2)}, u32[]{:S(2)}) collective-permute-start(bf16[256,512]{1,0:T(8,128)(2,1)S(1)} %get-tuple-element.35.refs_8_), channel_id=1, source_target_pairs={{0,8},{8,0},{16,24},{24,16},{1,9},{9,1},{17,25},{25,17},{2,10},{10... | collective-permute-start | bytes 786440 | tf_op jit(solution)/shard_map/ppermute | solution.py:353
  7.6 14.3 %collective-permute-start.1 = (bf16[128,1280]{1,0:T(8,128)(2,1)S(1)}, bf16[128,1280]{1,0:T(8,128)(2,1)S(1)}, u32[]{:S(2)}, u32[]{:S(2)}) collective-permute-start(bf16[128,1280]{1,0:T(8,128)(2,1)S(1)} %get-tuple-element.37), channel_id=1, source_target_pairs={{0,2},{2,0},{4,6},{6,4},{1,3},{3,1},{5,7},{7,5},{8,10},{10,8},{12,... | collective-permute-start | bytes 983048 | tf_op jit(solution)/shard_map/ppermute | solution.py:353
  9.1 15.6 %collective-permute-start.2 = (bf16[128,1280]{1,0:T(8,128)(2,1)S(1)}, bf16[128,1280]{1,0:T(8,128)(2,1)S(1)}, u32[]{:S(2)}, u32[]{:S(2)}) collective-permute-start(bf16[128,1280]{1,0:T(8,128)(2,1)S(1)} %get-tuple-element.38), channel_id=1, source_target_pairs={{0,4},{2,6},{4,0},{6,2},{1,5},{3,7},{5,1},{7,3},{8,12},{10,14},{12... | collective-permute-start | bytes 983048 | tf_op jit(solution)/shard_map/ppermute | solution.py:353
  10.6 14.1 %collective-permute-start.3 = (bf16[128,1280]{1,0:T(8,128)(2,1)S(1)}, bf16[128,1280]{1,0:T(8,128)(2,1)S(1)}, u32[]{:S(2)}, u32[]{:S(2)}) collective-permute-start(bf16[128,1280]{1,0:T(8,128)(2,1)S(1)} %get-tuple-element.39), channel_id=1, source_target_pairs={{0,6},{2,4},{4,2},{6,0},{1,7},{3,5},{5,3},{7,1},{8,14},{10,12},{12... | collective-permute-start | bytes 983048 | tf_op jit(solution)/shard_map/ppermute | solution.py:353
  18.1 7.4 %collective-permute-start.5 = (bf16[256,512]{1,0:T(8,128)(2,1)S(1)}, bf16[256,512]{1,0:T(8,128)(2,1)S(1)}, u32[]{:S(2)}, u32[]{:S(2)}) collective-permute-start(bf16[256,512]{1,0:T(8,128)(2,1)S(1)} %collective-permute-done.refs_10_), channel_id=1, source_target_pairs={{0,8},{8,0},{16,24},{24,16},{1,9},{9,1},{17,25},{25,17},{2,10},{10... | collective-permute-start | bytes 786440 | tf_op jit(solution)/shard_map/ppermute | solution.py:353
  18.7 33.2 %copy-start = (f32[3,1024]{1,0:T(4,128)S(1)}, f32[3,1024]{1,0:T(4,128)}, u32[]{:S(2)}) copy-start(f32[3,1024]{1,0:T(4,128)} %taps_ref.3) | copy-start | bytes 36868
  18.7 6.8 %collective-permute-start.6 = (bf16[128,1280]{1,0:T(8,128)(2,1)S(1)}, bf16[128,1280]{1,0:T(8,128)(2,1)S(1)}, u32[]{:S(2)}, u32[]{:S(2)}) collective-permute-start(bf16[128,1280]{1,0:T(8,128)(2,1)S(1)} %get-tuple-element.42.refs_0_), channel_id=1, source_target_pairs={{0,1},{1,0},{2,3},{3,2},{4,5},{5,4},{6,7},{7,6},{8,9},{9,8},{10,11... | collective-permute-start | bytes 983048 | tf_op jit(solution)/shard_map/ppermute | solution.py:353
  24.7 1.6 %collective-permute-start.7 = (bf16[128,1280]{1,0:T(8,128)(2,1)S(1)}, bf16[128,1280]{1,0:T(8,128)(2,1)S(1)}, u32[]{:S(2)}, u32[]{:S(2)}) collective-permute-start(bf16[128,1280]{1,0:T(8,128)(2,1)S(1)} %collective-permute-done.1.refs_1_), channel_id=1, source_target_pairs={{0,1},{1,0},{2,3},{3,2},{4,5},{5,4},{6,7},{7,6},{8,9},{9,8},{10,11... | collective-permute-start | bytes 983048 | tf_op jit(solution)/shard_map/ppermute | solution.py:353
  24.7 2.1 %collective-permute-start.8 = (bf16[128,1280]{1,0:T(8,128)(2,1)S(1)}, bf16[128,1280]{1,0:T(8,128)(2,1)S(1)}, u32[]{:S(2)}, u32[]{:S(2)}) collective-permute-start(bf16[128,1280]{1,0:T(8,128)(2,1)S(1)} %collective-permute-done.2.refs_2_), channel_id=1, source_target_pairs={{0,1},{1,0},{2,3},{3,2},{4,5},{5,4},{6,7},{7,6},{8,9},{9,8},{10,11... | collective-permute-start | bytes 983048 | tf_op jit(solution)/shard_map/ppermute | solution.py:353
  25.5 1.8 %collective-permute-start.9 = (bf16[128,1280]{1,0:T(8,128)(2,1)S(1)}, bf16[128,1280]{1,0:T(8,128)(2,1)S(1)}, u32[]{:S(2)}, u32[]{:S(2)}) collective-permute-start(bf16[128,1280]{1,0:T(8,128)(2,1)S(1)} %collective-permute-done.3.refs_3_), channel_id=1, source_target_pairs={{0,1},{1,0},{2,3},{3,2},{4,5},{5,4},{6,7},{7,6},{8,9},{9,8},{10,11... | collective-permute-start | bytes 983048 | tf_op jit(solution)/shard_map/ppermute | solution.py:353
  30.3 8.0 %collective-permute-start.11 = (bf16[64,1152]{1,0:T(8,128)(2,1)S(1)}, bf16[64,1152]{1,0:T(8,128)(2,1)S(1)}, u32[]{:S(2)}, u32[]{:S(2)}) collective-permute-start(bf16[64,1152]{1,0:T(8,128)(2,1)S(1)} %get-tuple-element.53), channel_id=1, source_target_pairs={{0,2},{2,0},{4,6},{6,4},{1,3},{3,1},{5,7},{7,5},{8,10},{10,8},{12,... | collective-permute-start | bytes 442376 | tf_op jit(solution)/shard_map/ppermute | solution.py:353
  31.6 7.7 %collective-permute-start.12 = (bf16[64,1152]{1,0:T(8,128)(2,1)S(1)}, bf16[64,1152]{1,0:T(8,128)(2,1)S(1)}, u32[]{:S(2)}, u32[]{:S(2)}) collective-permute-start(bf16[64,1152]{1,0:T(8,128)(2,1)S(1)} %get-tuple-element.54), channel_id=1, source_target_pairs={{0,4},{2,6},{4,0},{6,2},{1,5},{3,7},{5,1},{7,3},{8,12},{10,14},{12... | collective-permute-start | bytes 442376 | tf_op jit(solution)/shard_map/ppermute | solution.py:353
  33.0 7.4 %collective-permute-start.13 = (bf16[64,1152]{1,0:T(8,128)(2,1)S(1)}, bf16[64,1152]{1,0:T(8,128)(2,1)S(1)}, u32[]{:S(2)}, u32[]{:S(2)}) collective-permute-start(bf16[64,1152]{1,0:T(8,128)(2,1)S(1)} %get-tuple-element.55), channel_id=1, source_target_pairs={{0,6},{2,4},{4,2},{6,0},{1,7},{3,5},{5,3},{7,1},{8,14},{10,12},{12... | collective-permute-start | bytes 442376 | tf_op jit(solution)/shard_map/ppermute | solution.py:353
  33.9 4.4 %collective-permute-start.10 = (bf16[2,512]{1,0:T(2,128)(2,1)S(1)}, bf16[2,512]{1,0:T(2,128)(2,1)S(1)}, u32[]{:S(2)}, u32[]{:S(2)}) collective-permute-start(bf16[2,512]{1,0:T(2,128)(2,1)S(1)} %slice.3), channel_id=1, source_target_pairs={{0,2},{2,4},{4,6},{6,8},{8,10},{10,12},{12,14},{14,16},{16,18},{18... | collective-permute-start | bytes 6152 | tf_op jit(solution)/shard_map/ppermute | solution.py:435
  40.5 5.5 %collective-permute-start.14 = (bf16[16,1536]{1,0:T(8,128)(2,1)S(1)}, bf16[16,1536]{1,0:T(8,128)(2,1)S(1)}, u32[]{:S(2)}, u32[]{:S(2)}) collective-permute-start(bf16[16,1536]{1,0:T(8,128)(2,1)S(1)} %get-tuple-element.62), channel_id=1, source_target_pairs={{0,8},{8,0},{16,24},{24,16},{1,9},{9,1},{17,25},{25,17},{2,10},{10... | collective-permute-start | bytes 147464 | tf_op jit(solution)/shard_map/ppermute | solution.py:353
  42.6 6.5 %collective-permute-start.15 = (bf16[16,1536]{1,0:T(8,128)(2,1)S(1)}, bf16[16,1536]{1,0:T(8,128)(2,1)S(1)}, u32[]{:S(2)}, u32[]{:S(2)}) collective-permute-start(bf16[16,1536]{1,0:T(8,128)(2,1)S(1)} %get-tuple-element.63), channel_id=1, source_target_pairs={{0,16},{8,24},{16,0},{24,8},{1,17},{9,25},{17,1},{25,9},{2,18},{10... | collective-permute-start | bytes 147464 | tf_op jit(solution)/shard_map/ppermute | solution.py:353
  46.0 5.9 %collective-permute-start.16 = (bf16[16,1536]{1,0:T(8,128)(2,1)S(1)}, bf16[16,1536]{1,0:T(8,128)(2,1)S(1)}, u32[]{:S(2)}, u32[]{:S(2)}) collective-permute-start(bf16[16,1536]{1,0:T(8,128)(2,1)S(1)} %get-tuple-element.64), channel_id=1, source_target_pairs={{0,24},{8,16},{16,8},{24,0},{1,25},{9,17},{17,9},{25,1},{2,26},{10... | collective-permute-start | bytes 147464 | tf_op jit(solution)/shard_map/ppermute | solution.py:353
